TPU v7x, 32 devices: a whole 2x2x4 slice. The times are simulated.
32 devices in a mesh: wide: 16 (over z, x, core), narrow: 2 (over y).
Axes of the slice: x: 2, y: 2, z: 4, core: 2. Of those that a mesh axis runs over, the one named last changes fastest.
Arguments:
- tokens: bfloat16 [32768, 768], P(('wide', 'narrow')), may hold values from -6 to 6
- patch_grid: int32 [64, 4, 2], P(('wide', 'narrow')), may hold values from 8 to 11
- qkv_rows: bfloat16 [13824, 128], P(('wide', 'narrow')), may hold values from -0.21875 to 0.21875
- proj_rows: bfloat16 [4608, 128], P(('wide', 'narrow')), may hold values from -0.625 to 0.625
- fc1_rows: bfloat16 [18432, 128], P(('wide', 'narrow')), may hold values from -0.21875 to 0.21875
- fc2_rows: bfloat16 [18432, 128], P(('wide', 'narrow')), may hold values from -0.15625 to 0.15625
- norm_gain: float32 [2, 768], replicated, may hold values from 0.5 to 1.5
- norm_bias: float32 [2, 768], replicated, may hold values from -2 to 2
- qv_bias: float32 [2, 768], replicated, may hold values from -2 to 2
- proj_bias: float32 [768], replicated, may hold values from -2 to 2
- fc1_bias: float32 [3072], replicated, may hold values from -2 to 2
- fc2_bias: float32 [768], replicated, may hold values from -2 to 2
- layer_scale: float32 [2, 768], replicated, may hold values from 0.1 to 0.4
- cotangent: bfloat16 [32768, 768], P(('wide', 'narrow')), may hold values from -6 to 6
Outputs:
- layer_out: bfloat16 [32768, 768], P(('wide', 'narrow'))
- input_grad: float32 [32768, 768], P(('wide', 'narrow'))
- qkv_grad: float32 [13824, 128], P(('wide', 'narrow'))
- proj_grad: float32 [4608, 128], P(('wide', 'narrow'))
- fc1_grad: float32 [18432, 128], P(('wide', 'narrow'))
- fc2_grad: float32 [18432, 128], P(('wide', 'narrow'))
- gain_grad: float32 [2, 768], replicated
- norm_bias_grad: float32 [2, 768], replicated
- qv_bias_grad: float32 [2, 768], replicated
- proj_bias_grad: float32 [768], replicated
- fc1_bias_grad: float32 [3072], replicated
- fc2_bias_grad: float32 [768], replicated
- scale_grad: float32 [2, 768], replicated
All inputs are finite; a program needn't handle non-finite values.
Results may differ from a plain program's by a relative error of at most 0.0087.
Values may be sent and summed in bfloat16 or wider, within the bound.
No kernel may reach another device: no remote copies, remote signals or barrier semaphores. Data moves between devices by JAX's collectives and lax.ppermute only.
A program may use at most 192 MiB of HBM per device.

v0:
```python
from functools import partial

import jax
import jax.numpy as jnp
from jax import lax
from jax.sharding import PartitionSpec as P

H = 12
PREFIX = 5


EPSILON = 1e-06
NEGATIVE = -1e30


def layout(patch_grid, pack):
    lengths = PREFIX + patch_grid[:, :, 0] * patch_grid[:, :, 1]
    image_ends = jnp.cumsum(lengths, axis=1)
    position = lax.iota(jnp.int32, pack)
    segment = jnp.sum((position[None, :, None] >= image_ends[:, None, :]).astype(jnp.int32), axis=2)
    usable = segment < patch_grid.shape[1]
    joined = (segment[:, :, None] == segment[:, None, :]) & usable[:, None, :]
    itself = position[:, None] == position[None, :]
    return (usable, joined | itself[None])


def normalize(inputs, factor, offset):
    average = jnp.mean(inputs, axis=-1, keepdims=True)
    centered = inputs - average
    variance = jnp.mean(centered * centered, axis=-1, keepdims=True)
    inverse = lax.rsqrt(variance + EPSILON)
    scaled = centered * inverse
    return (scaled * factor + offset, scaled, inverse)


def normalize_back(upstream, scaled, inverse, factor):
    factor_grad = jnp.sum(upstream * scaled, axis=0)
    offset_grad = jnp.sum(upstream, axis=0)
    scaled_grad = upstream * factor
    inner = jnp.mean(scaled_grad, axis=-1, keepdims=True) + scaled * jnp.mean(
        scaled_grad * scaled, axis=-1, keepdims=True
    )
    return (inverse * (scaled_grad - inner), factor_grad, offset_grad)


def shape_weights(gathered, width, hidden_width):
    return (
        gathered[0].reshape(width, 3 * width),
        gathered[1].reshape(width, width),
        gathered[2].reshape(width, hidden_width),
        gathered[3].reshape(hidden_width, width),
    )


def body(
    tokens,
    patch_grid,
    qkv_rows,
    proj_rows,
    fc1_rows,
    fc2_rows,
    norm_gain,
    norm_bias,
    qv_bias,
    proj_bias,
    fc1_bias,
    fc2_bias,
    layer_scale,
    cotangent,
):
    width = tokens.shape[1]
    packs = patch_grid.shape[0]
    pack = tokens.shape[0] // packs
    head_size = width // H
    hidden_width = fc1_bias.shape[0]
    row_width = qkv_rows.shape[1]
    factor = head_size ** (-0.5)
    usable_rows, joined = layout(patch_grid, pack)
    usable = usable_rows.reshape(-1, 1).astype(jnp.float32)
    allowed = joined[:, None]
    gathered = (
        lax.all_gather(qkv_rows, ("wide", "narrow"), axis=0, tiled=True),
        lax.all_gather(proj_rows, ("wide", "narrow"), axis=0, tiled=True),
        lax.all_gather(fc1_rows, ("wide", "narrow"), axis=0, tiled=True),
        lax.all_gather(fc2_rows, ("wide", "narrow"), axis=0, tiled=True),
    )
    qkv_w, proj_w, fc1_w, fc2_w = shape_weights(gathered, width, hidden_width)
    inputs = tokens.astype(jnp.float32) * usable
    normed, scaled_one, inverse_one = normalize(inputs, norm_gain[0], norm_bias[0])
    normed_one = normed.astype(jnp.bfloat16)
    offset = jnp.concatenate([qv_bias[0], jnp.zeros_like(qv_bias[0]), qv_bias[1]])
    projected = (jnp.dot(normed_one, qkv_w, preferred_element_type=jnp.float32) + offset).astype(
        jnp.bfloat16
    )
    head_shape = (packs, pack, H, head_size)
    queries = projected[:, :width].reshape(head_shape)
    key_rows = projected[:, width : 2 * width].reshape(head_shape)
    values = projected[:, 2 * width :].reshape(head_shape)
    scores = (
        jnp.einsum("pqhd,pkhd->phqk", queries, key_rows, preferred_element_type=jnp.float32)
        * factor
    )
    masked = jnp.where(allowed, scores, NEGATIVE)
    row_top = jnp.max(masked, axis=-1, keepdims=True)
    exponent = jnp.exp(masked - row_top)
    row_total = jnp.sum(exponent, axis=-1, keepdims=True)
    log_total = row_top + jnp.log(row_total)
    weighted = (exponent / row_total).astype(jnp.bfloat16)
    attended = jnp.einsum("phqk,pkhd->pqhd", weighted, values, preferred_element_type=jnp.float32)
    attended = attended.reshape(-1, width).astype(jnp.bfloat16)
    branch_one = jnp.dot(attended, proj_w, preferred_element_type=jnp.float32) + proj_bias
    middle = inputs + layer_scale[0] * branch_one
    normed, scaled_two, inverse_two = normalize(middle, norm_gain[1], norm_bias[1])
    normed_two = normed.astype(jnp.bfloat16)
    hidden = jnp.dot(normed_two, fc1_w, preferred_element_type=jnp.float32) + fc1_bias
    activated, gelu_pull = jax.vjp(partial(jax.nn.gelu, approximate=False), hidden)
    activated = activated.astype(jnp.bfloat16)
    branch_two = jnp.dot(activated, fc2_w, preferred_element_type=jnp.float32) + fc2_bias
    layer_out = (usable * (middle + layer_scale[1] * branch_two)).astype(jnp.bfloat16)
    again = (
        lax.all_gather(qkv_rows, ("wide", "narrow"), axis=0, tiled=True),
        lax.all_gather(proj_rows, ("wide", "narrow"), axis=0, tiled=True),
        lax.all_gather(fc1_rows, ("wide", "narrow"), axis=0, tiled=True),
        lax.all_gather(fc2_rows, ("wide", "narrow"), axis=0, tiled=True),
    )
    qkv_w, proj_w, fc1_w, fc2_w = shape_weights(again, width, hidden_width)
    upstream = cotangent.astype(jnp.float32) * usable
    scale_two_grad = jnp.sum(upstream * branch_two, axis=0)
    branch_two_grad = (layer_scale[1] * upstream).astype(jnp.bfloat16)
    fc2_bias_grad = jnp.sum(branch_two_grad.astype(jnp.float32), axis=0)
    fc2_grad = jnp.einsum(
        "tf,td->fd", activated, branch_two_grad, preferred_element_type=jnp.float32
    )
    activated_grad = jnp.einsum(
        "td,fd->tf", branch_two_grad, fc2_w, preferred_element_type=jnp.float32
    )
    hidden_grad = gelu_pull(activated_grad)[0].astype(jnp.bfloat16)
    fc1_bias_grad = jnp.sum(hidden_grad.astype(jnp.float32), axis=0)
    fc1_grad = jnp.einsum("td,tf->df", normed_two, hidden_grad, preferred_element_type=jnp.float32)
    normed_two_grad = jnp.einsum(
        "tf,df->td", hidden_grad, fc1_w, preferred_element_type=jnp.float32
    )
    middle_norm_grad, gain_two_grad, offset_two_grad = normalize_back(
        normed_two_grad, scaled_two, inverse_two, norm_gain[1]
    )
    middle_grad = upstream + middle_norm_grad
    scale_one_grad = jnp.sum(middle_grad * branch_one, axis=0)
    branch_one_grad = (layer_scale[0] * middle_grad).astype(jnp.bfloat16)
    proj_bias_grad = jnp.sum(branch_one_grad.astype(jnp.float32), axis=0)
    proj_grad = jnp.einsum(
        "td,te->de", attended, branch_one_grad, preferred_element_type=jnp.float32
    )
    attended_grad = jnp.einsum(
        "te,de->td", branch_one_grad, proj_w, preferred_element_type=jnp.float32
    )
    attended_grad = attended_grad.astype(jnp.bfloat16).reshape(head_shape)
    scores = (
        jnp.einsum("pqhd,pkhd->phqk", queries, key_rows, preferred_element_type=jnp.float32)
        * factor
    )
    masked = jnp.where(allowed, scores, NEGATIVE)
    probability = jnp.exp(masked - log_total)
    probability_grad = jnp.einsum(
        "pqhd,pkhd->phqk", attended_grad, values, preferred_element_type=jnp.float32
    )
    inner_total = jnp.sum(probability_grad * probability, axis=-1, keepdims=True)
    score_grad = (probability * (probability_grad - inner_total)).astype(jnp.bfloat16)
    query_grad = (
        jnp.einsum("phqk,pkhd->pqhd", score_grad, key_rows, preferred_element_type=jnp.float32)
        * factor
    )
    key_grad = (
        jnp.einsum("phqk,pqhd->pkhd", score_grad, queries, preferred_element_type=jnp.float32)
        * factor
    )
    value_grad = jnp.einsum(
        "phqk,pqhd->pkhd",
        probability.astype(jnp.bfloat16),
        attended_grad,
        preferred_element_type=jnp.float32,
    )
    projected_grad = jnp.concatenate(
        [query_grad.reshape(-1, width), key_grad.reshape(-1, width), value_grad.reshape(-1, width)],
        axis=1,
    ).astype(jnp.bfloat16)
    projected_sums = jnp.sum(projected_grad.astype(jnp.float32), axis=0)
    qv_bias_grad = jnp.stack([projected_sums[:width], projected_sums[2 * width :]])
    qkv_grad = jnp.einsum(
        "td,te->de", normed_one, projected_grad, preferred_element_type=jnp.float32
    )
    normed_one_grad = jnp.einsum(
        "te,de->td", projected_grad, qkv_w, preferred_element_type=jnp.float32
    )
    input_norm_grad, gain_one_grad, offset_one_grad = normalize_back(
        normed_one_grad, scaled_one, inverse_one, norm_gain[0]
    )
    input_grad = usable * (middle_grad + input_norm_grad)
    qkv_flat = qkv_grad.reshape(-1, row_width)
    proj_flat = proj_grad.reshape(-1, row_width)
    fc1_flat = fc1_grad.reshape(-1, row_width)
    fc2_flat = fc2_grad.reshape(-1, row_width)
    owned = (
        lax.psum_scatter(qkv_flat, ("wide", "narrow"), scatter_dimension=0, tiled=True),
        lax.psum_scatter(proj_flat, ("wide", "narrow"), scatter_dimension=0, tiled=True),
        lax.psum_scatter(fc1_flat, ("wide", "narrow"), scatter_dimension=0, tiled=True),
        lax.psum_scatter(fc2_flat, ("wide", "narrow"), scatter_dimension=0, tiled=True),
    )
    gain_grad = jnp.stack([gain_one_grad, gain_two_grad])
    norm_bias_grad = jnp.stack([offset_one_grad, offset_two_grad])
    scale_grad = jnp.stack([scale_one_grad, scale_two_grad])
    summed = lax.psum(
        (
            gain_grad,
            norm_bias_grad,
            qv_bias_grad,
            proj_bias_grad,
            fc1_bias_grad,
            fc2_bias_grad,
            scale_grad,
        ),
        ("wide", "narrow"),
    )
    return (
        layer_out,
        input_grad,
        owned[0],
        owned[1],
        owned[2],
        owned[3],
        summed[0],
        summed[1],
        summed[2],
        summed[3],
        summed[4],
        summed[5],
        summed[6],
    )


def solution(mesh):
    return jax.shard_map(
        body,
        mesh=mesh,
        in_specs=(
            P(("wide", "narrow"), None),
            P(("wide", "narrow"), None, None),
            P(("wide", "narrow"), None),
            P(("wide", "narrow"), None),
            P(("wide", "narrow"), None),
            P(("wide", "narrow"), None),
            P(),
            P(),
            P(),
            P(),
            P(),
            P(),
            P(),
            P(("wide", "narrow"), None),
        ),
        out_specs=(
            P(("wide", "narrow"), None),
            P(("wide", "narrow"), None),
            P(("wide", "narrow"), None),
            P(("wide", "narrow"), None),
            P(("wide", "narrow"), None),
            P(("wide", "narrow"), None),
            P(),
            P(),
            P(),
            P(),
            P(),
            P(),
            P(),
        ),
        check_vma=False,
    )
```

profile of v0, /device:TPU:0, one launch (start us, length us, event | category | flops | bytes accessed | tf_op | source)
XLA Modules:
  0.0 865.4 jit_solution(9910549944054925779)
XLA Ops:
  16.0 51.8 %all-gather.7.cloned.1.call-done = bf16[4608,128]{1,0:T(8,128)(2,1)} async-done(((bf16[144,128]{1,0:T(8,128)(2,1)}), bf16[4608,128]{1,0:T(8,128)(2,1)}) %all-gather.7.cloned.1.call-update) | async-done | bytes 1179664 | tf_op jit(solution)/shard_map/all_gather | solution.py:83
  71.2 58.7 %all-gather.5.cloned.1.call-done = bf16[13824,128]{1,0:T(8,128)(2,1)} async-done(((bf16[432,128]{1,0:T(8,128)(2,1)}), bf16[13824,128]{1,0:T(8,128)(2,1)}) %all-gather.5.cloned.1.call-update) | async-done | bytes 3538960 | tf_op jit(solution)/shard_map/all_gather | solution.py:82
  161.1 11.7 %fusion.12 = (f32[2,12,512]{2,1,0:T(8,128)S(1)}, f32[2,12,512,512]{2,3,1,0:T(8,128)}) fusion(pred[2,512,512]{1,2,0:T(8,128)(4,1)} %and_or_fusion, bf16[2,512,12,64]{1,0,3,2:T(2,128)(2,1)S(1)} %reshape.188, bf16[2,512,12,64]{1,0,3,2:T(2,128)(2,1)S(1)} %reshape.187), kind=kOutput, calls=%fused_computation.31 | convolution fusion | flops 824168448 | bytes 28884992 | tf_op jit(solution)/shard_map/pqhd,pkhd->phqk/dot_general | solution.py:100
  172.8 11.5 %fusion = f32[2,12,512]{2,1,0:T(8,128)S(1)} fusion(f32[2,12,512]{2,1,0:T(8,128)S(1)} %get-tuple-element.56, f32[2,12,512,512]{2,3,1,0:T(8,128)} %get-tuple-element.57, pred[2,512,512]{1,2,0:T(8,128)(4,1)S(1)} %copy-done.11), kind=kLoop, calls=%fused_computation.6 | loop fusion | flops 25153536 | bytes 25788416 | tf_op jit(solution)/shard_map/reduce_sum | solution.py:106
  184.4 12.2 %fusion.25 = bf16[2,512,12,64]{1,3,2,0:T(8,128)(2,1)S(1)} fusion(f32[2,12,512]{2,1,0:T(8,128)S(1)} %fusion, f32[2,12,512]{2,1,0:T(8,128)S(1)} %get-tuple-element.56, f32[2,12,512,512]{2,3,1,0:T(8,128)} %get-tuple-element.57, pred[2,512,512]{1,2,0:T(8,128)(4,1)S(1)} %copy-done.11, bf16[2,512,12,64]{1,0,3,2:T(2,128)(2,1)S(1)} %copy-done.14), kind=kOutput, calls=%fused_computation.67 | convolution fusion | flops 837550080 | bytes 28934144 | tf_op jit(solution)/shard_map/phqk,pkhd->pqhd/dot_general | solution.py:109
  211.0 36.2 %multiply_convert_fusion.1 = (bf16[1024,3072]{1,0:T(8,128)(2,1)}, f32[1024,3072]{1,0:T(8,128)}, f32[1024,3072]{1,0:T(8,128)}) fusion(f32[3072]{0:T(1024)S(1)} %copy-done.38, bf16[768,3072]{1,0:T(8,128)(2,1)} %reshape.190, f32[1024,768]{1,0:T(8,128)S(1)} %get-tuple-element.47, f32[768]{0:T(1024)S(1)} %get-tuple-element.27, f32[768]{0:T(1024)S(1)} %get-tuple-element.67, ...), kind=kOutput, calls=%fused_computation.14 | convolution fusion | flops 5043388416 | bytes 39348224 | tf_op jit(solution)/shard_map/dot_general | solution.py:115
  247.2 13.4 %all-gather.11.cloned.1.call-done = bf16[18432,128]{1,0:T(8,128)(2,1)} async-done(((bf16[576,128]{1,0:T(8,128)(2,1)}), bf16[18432,128]{1,0:T(8,128)(2,1)}) %all-gather.11.cloned.1.call-update) | async-done | bytes 4718608 | tf_op jit(solution)/shard_map/all_gather | solution.py:85
  260.6 9.2 %reshape.191 = bf16[3072,768]{1,0:T(8,128)(2,1)} reshape(bf16[18432,128]{1,0:T(8,128)(2,1)} %all-gather.11.cloned.1.call-done) | data formatting | bytes 9437184 | tf_op jit(solution)/shard_map/reshape | solution.py:51
  269.8 19.2 %convert_reduce_fusion = (f32[3072]{0:T(1024)}, bf16[1024,3072]{1,0:T(8,128)(2,1)}) fusion(f32[1024,3072]{1,0:T(8,128)} %get-tuple-element.45, bf16[3072,768]{1,0:T(8,128)(2,1)} %reshape.191, bf16[1024,768]{1,0:T(8,128)(2,1)} %param.27, f32[768]{0:T(1024)S(1)} %copy-done.35, f32[1024]{0:T(1024)S(1)} %bitcast.75, f32[1024,3072]{1,0:T(8,128)} %get-tuple-element.59, ...), kind=kOutput, calls=%fused_computation.11 | convolution fusion | flops 4888458240 | bytes 37780480 | tf_op jit(solution)/shard_map/td,fd->tf/dot_general | solution.py:134
  289.0 9.4 %multiply_reduce_fusion.3 = (f32[768]{0:T(1024)S(1)}, f32[1024]{0:T(1024)S(1)}, f32[1024]{0:T(1024)S(1)}, f32[768]{0:T(1024)S(1)}, f32[1024,768]{1,0:T(8,128)S(1)}) fusion(f32[1024,768]{1,0:T(8,128)S(1)} %get-tuple-element.47, f32[1024]{0:T(1024)S(1)} %add_rsqrt_fusion, f32[1024]{0:T(1024)S(1)} %broadcast_multiply_fusion.4, f32[768]{0:T(1024)S(1)} %get-tuple-element.67, ...), kind=kOutput, calls=%fused_computation.36 | convolution fusion | flops 4838912000 | bytes 17327104 | tf_op jit(solution)/shard_map/tf,df->td/dot_general | solution.py:140
  314.4 12.7 %fusion.20 = bf16[2,512,12,64]{1,3,2,0:T(8,128)(2,1)} fusion(f32[2,12,512]{2,1,0:T(8,128)S(1)} %log_add_fusion, f32[2,12,512,512]{2,3,1,0:T(8,128)} %get-tuple-element.57, pred[2,512,512]{1,2,0:T(8,128)(4,1)} %and_or_fusion, bf16[2,512,12,64]{1,0,3,2:T(2,128)(2,1)} %reshape.192), kind=kOutput, calls=%fused_computation.64 | convolution fusion | flops 831258624 | bytes 28884992 | tf_op jit(solution)/shard_map/phqk,pqhd->pkhd/dot_general | solution.py:176
  327.1 21.0 %multiply_reduce_fusion = (f32[2,12,512]{2,1,0:T(8,128)S(1)}, f32[2,12,512,512]{2,3,1,0:T(8,128)}) fusion(f32[2,12,512]{2,1,0:T(8,128)S(1)} %log_add_fusion, f32[2,12,512,512]{2,3,1,0:T(8,128)} %get-tuple-element.57, pred[2,512,512]{1,2,0:T(8,128)(4,1)} %and_or_fusion, bf16[2,512,12,64]{1,0,3,2:T(2,128)(2,1)} %reshape.186, bf16[2,512,12,64]{1,0,3,2:T(2,128)(2,1)} %reshape.192), kind=kOutput, calls=%fused_computation.1 | convolution fusion | flops 836751360 | bytes 54099968 | tf_op jit(solution)/shard_map/pqhd,pkhd->phqk/dot_general | solution.py:163
  355.0 18.1 %multiply_convert_fusion = bf16[2,12,512,512]{2,3,1,0:T(8,128)(2,1)S(1)} fusion(f32[2,12,512,512]{2,3,1,0:T(8,128)} %get-tuple-element.62, f32[2,12,512]{2,1,0:T(8,128)S(1)} %get-tuple-element.61, f32[2,12,512]{2,1,0:T(8,128)S(1)} %log_add_fusion, f32[2,12,512,512]{2,3,1,0:T(8,128)} %get-tuple-element.57, pred[2,512,512]{1,2,0:T(8,128)(4,1)S(1)} %copy-done.12), kind=kLoop, calls=%fused_computation | loop fusion | flops 37748736 | bytes 63537152 | tf_op jit(solution)/shard_map/convert_element_type | solution.py:167
  379.7 8.6 fusion.24
  408.2 10.7 %fusion.41 = f32[768,3072]{1,0:T(8,128)} fusion(bf16[1024,3072]{1,0:T(8,128)(2,1)} %get-tuple-element.65, f32[1024,768]{1,0:T(8,128)S(1)} %get-tuple-element.47, f32[768]{0:T(1024)S(1)} %get-tuple-element.27, f32[768]{0:T(1024)S(1)} %get-tuple-element.67, f32[1024]{0:T(1024)S(1)} %add_rsqrt_fusion, f32[1024]{0:T(1024)S(1)} %broadcast_multiply_fusion.4), kind=kOutput, calls=%fused_computation.114 | convolution fusion | flops 4835770368 | bytes 18888704 | tf_op jit(solution)/shard_map/td,tf->df/dot_general | solution.py:139
  418.9 11.0 %reshape.198 = f32[18432,128]{1,0:T(8,128)} reshape(f32[768,3072]{1,0:T(8,128)} %fusion.41) | data formatting | bytes 18874368 | tf_op jit(solution)/shard_map/reshape | solution.py:200
  430.0 10.2 %fusion.40 = f32[3072,768]{1,0:T(8,128)} fusion(bf16[1024,3072]{1,0:T(8,128)(2,1)} %get-tuple-element.44, bf16[1024,768]{1,0:T(8,128)(2,1)} %param.27, f32[768]{0:T(1024)S(1)} %copy-done.35, f32[1024]{0:T(1024)S(1)} %bitcast.78), kind=kOutput, calls=%fused_computation.113 | convolution fusion | flops 4834983936 | bytes 17308672 | tf_op jit(solution)/shard_map/tf,td->fd/dot_general | solution.py:131
  440.2 10.8 %reshape.199 = f32[18432,128]{1,0:T(8,128)} reshape(f32[3072,768]{1,0:T(8,128)} %fusion.40) | data formatting | bytes 18874368 | tf_op jit(solution)/shard_map/reshape | solution.py:201
  451.1 8.7 %fusion.48 = f32[1024,768]{1,0:T(8,128)S(1)} fusion(bf16[1024,3072]{1,0:T(8,128)(2,1)} %get-tuple-element.44, bf16[3072,768]{1,0:T(8,128)(2,1)} %reshape.191), kind=kOutput, calls=%fused_computation.120 | convolution fusion | flops 4831838208 | bytes 14155776 | tf_op jit(solution)/shard_map/dot_general | solution.py:118
  459.8 9.5 %multiply_reduce_fusion.4 = (f32[768]{0:T(1024)S(1)}, f32[1024]{0:T(1024)S(1)}, f32[1024]{0:T(1024)S(1)}, f32[768]{0:T(1024)S(1)}, f32[768]{0:T(1024)S(1)}, /*in...) fusion(bf16[1024,768]{1,0:T(8,128)(2,1)S(1)} %copy-done.10, f32[1024]{0:T(1024)S(1)} %copy-done.28, ...), kind=kOutput, calls=%fused_computation.37 | convolution fusion | flops 3642747904 | bytes 22455296 | tf_op jit(solution)/shard_map/te,de->td/dot_general | solution.py:191
  470.2 41.1 %all-reduce = (f32[2,768]{1,0:T(2,128)}, f32[2,768]{1,0:T(2,128)}, f32[2,768]{1,0:T(2,128)}, f32[768]{0:T(1024)}, f32[3072]{0:T(1024)}, /*index=5*/f32[768]{0:T(1024)}, f32[2,768]{1,0:T(2,128)}) all-reduce(f32[2,768]{1,0:T(2,128)S(1)} %pad_maximum_fusion.1, ...), channel_id=1, replica_groups=mesh['wide'=16,'narrow'=2] {'wide','narrow'}, use_global_device_ids=true, to_apply=%region_19.20 | all-reduce | flops 10752 | bytes 86016 | tf_op jit(solution)/shard_map/psum | solution.py:211
  515.5 59.3 %reduce-scatter.5.cloned.1.call-done = f32[432,128]{1,0:T(8,128)} async-done(((f32[13824,128]{1,0:T(8,128)}), f32[432,128]{1,0:T(8,128)}) %reduce-scatter.5.cloned.1.call-update) | async-done | bytes 221200 | tf_op jit(solution)/shard_map/reduce_scatter | solution.py:203
  574.9 141.2 %reduce-scatter.9.cloned.1.call-done = f32[576,128]{1,0:T(8,128)} async-done(((f32[18432,128]{1,0:T(8,128)}), f32[576,128]{1,0:T(8,128)}) %reduce-scatter.9.cloned.1.call-update) | async-done | bytes 294928 | tf_op jit(solution)/shard_map/reduce_scatter | solution.py:205
  716.1 142.3 %reduce-scatter.11.cloned.1.call-done = f32[576,128]{1,0:T(8,128)} async-done(((f32[18432,128]{1,0:T(8,128)}), f32[576,128]{1,0:T(8,128)}) %reduce-scatter.11.cloned.1.call-update) | async-done | bytes 294928 | tf_op jit(solution)/shard_map/reduce_scatter | solution.py:206
  (175 shorter events, 111.6 us)
Async XLA Ops:
  7.2 60.6 %all-gather.7.cloned.1.call-start = ((), (), s32[]{:S(2)}) async-start(), calls=%async_computation.5 | async-start | bytes 1216512 | tf_op jit(solution)/shard_map/all_gather | solution.py:83
  8.0 122.0 %all-gather.5.cloned.1.call-start = ((), (), s32[]{:S(2)}) async-start(), calls=%async_computation.4 | async-start | bytes 3649536 | tf_op jit(solution)/shard_map/all_gather | solution.py:82
  8.7 194.0 %all-gather.9.cloned.1.call-start = ((), (), s32[]{:S(2)}) async-start(), calls=%async_computation.6 | async-start | bytes 4866048 | tf_op jit(solution)/shard_map/all_gather | solution.py:84
  9.4 251.1 %all-gather.11.cloned.1.call-start = ((), (), s32[]{:S(2)}) async-start(), calls=%async_computation.7 | async-start | bytes 4866048 | tf_op jit(solution)/shard_map/all_gather | solution.py:85
  10.0 505.5 %reduce-scatter.7.cloned.1.call-start = ((), (), s32[]{:S(2)}) async-start(), calls=%async_computation.9 | async-start | bytes 2433024 | tf_op jit(solution)/shard_map/reduce_scatter | solution.py:204
  13.2 124.3 %copy-start.23 = (f32[1024]{0:T(1024)}, f32[1024]{0:T(1024)S(1)}, u32[]{:S(2)}) copy-start(f32[1024]{0:T(1024)S(1)} %broadcast_multiply_fusion.5) | copy-start | bytes 12292
  14.0 123.6 %copy-start.27 = (f32[1024]{0:T(1024)}, f32[1024]{0:T(1024)S(1)}, u32[]{:S(2)}) copy-start(f32[1024]{0:T(1024)S(1)} %add_rsqrt_fusion.1) | copy-start | bytes 12292
  14.7 122.9 %copy-start.25 = (f32[768]{0:T(1024)}, f32[768]{0:T(1024)S(1)}, u32[]{:S(2)}) copy-start(f32[768]{0:T(1024)S(1)} %get-tuple-element.66) | copy-start | bytes 9220
  14.7 122.8 %copy-start.36 = (f32[768]{0:T(1024)}, f32[768]{0:T(1024)S(1)}, u32[]{:S(2)}) copy-start(f32[768]{0:T(1024)S(1)} %get-tuple-element.28) | copy-start | bytes 9220
  161.1 11.7 %copy-start.5 = (bf16[2,512,12,64]{1,0,3,2:T(2,128)(2,1)}, bf16[2,512,12,64]{1,0,3,2:T(2,128)(2,1)S(1)}, u32[]{:S(2)}) copy-start(bf16[2,512,12,64]{1,0,3,2:T(2,128)(2,1)S(1)} %reshape.187) | copy-start | bytes 4718596
  161.1 11.7 %copy-start.11 = (pred[2,512,512]{1,2,0:T(8,128)(4,1)S(1)}, pred[2,512,512]{1,2,0:T(8,128)(4,1)}, u32[]{:S(2)}) copy-start(pred[2,512,512]{1,2,0:T(8,128)(4,1)} %and_or_fusion) | copy-start | bytes 1572868
  172.8 11.6 %copy-start.14 = (bf16[2,512,12,64]{1,0,3,2:T(2,128)(2,1)S(1)}, bf16[2,512,12,64]{1,0,3,2:T(2,128)(2,1)}, u32[]{:S(2)}) copy-start(bf16[2,512,12,64]{1,0,3,2:T(2,128)(2,1)} %reshape.186) | copy-start | bytes 4718596
  247.2 22.6 %copy-start.35 = (f32[768]{0:T(1024)S(1)}, f32[768]{0:T(1024)}, u32[]{:S(2)}) copy-start(f32[768]{0:T(1024)} %get-tuple-element.23) | copy-start | bytes 9220
  289.0 9.4 %copy-start.16 = (f32[1024,768]{1,0:T(8,128)S(1)}, f32[1024,768]{1,0:T(8,128)}, u32[]{:S(2)}) copy-start(f32[1024,768]{1,0:T(8,128)} %get-tuple-element.58) | copy-start | bytes 9437188
  289.0 9.4 %copy-start.17 = (bf16[1024,768]{1,0:T(8,128)(2,1)S(1)}, bf16[1024,768]{1,0:T(8,128)(2,1)}, u32[]{:S(2)}) copy-start(bf16[1024,768]{1,0:T(8,128)(2,1)} %param.27) | copy-start | bytes 4718596
  351.4 223.5 %reduce-scatter.5.cloned.1.call-start = ((), (), s32[]{:S(2)}) async-start(), calls=%async_computation.8 | async-start | bytes 7299072 | tf_op jit(solution)/shard_map/reduce_scatter | solution.py:203
  355.0 18.1 %copy-start.4 = (bf16[2,512,12,64]{1,0,3,2:T(2,128)(2,1)S(1)}, bf16[2,512,12,64]{1,0,3,2:T(2,128)(2,1)}, u32[]{:S(2)}) copy-start(bf16[2,512,12,64]{1,0,3,2:T(2,128)(2,1)} %copy-done.3) | copy-start | bytes 4718596
  408.1 307.9 %reduce-scatter.9.cloned.1.call-start = ((), (), s32[]{:S(2)}) async-start(), calls=%async_computation.10 | async-start | bytes 9732096 | tf_op jit(solution)/shard_map/reduce_scatter | solution.py:205
  429.9 428.4 %reduce-scatter.11.cloned.1.call-start = ((), (), s32[]{:S(2)}) async-start(), calls=%async_computation.11 | async-start | bytes 9732096 | tf_op jit(solution)/shard_map/reduce_scatter | solution.py:206
  451.0 18.4 %slice-start = ((s8[4718592]{0:T(1024)(128)(4,1)}), s8[4194304]{0:T(1024)(128)(4,1)S(1)}, s32[]{:S(2)}) async-start(s8[4718592]{0:T(1024)(128)(4,1)} %bitcast.60), calls=%async_computation.12 | async-start | bytes 8388608
  451.1 8.7 %copy-start.10 = (bf16[1024,768]{1,0:T(8,128)(2,1)S(1)}, bf16[1024,768]{1,0:T(8,128)(2,1)}, u32[]{:S(2)}) copy-start(bf16[1024,768]{1,0:T(8,128)(2,1)} %param.14) | copy-start | bytes 4718596
  451.1 8.7 %copy-start.15 = (bf16[768,2304]{1,0:T(8,128)(2,1)S(1)}, bf16[768,2304]{1,0:T(8,128)(2,1)}, u32[]{:S(2)}) copy-start(bf16[768,2304]{1,0:T(8,128)(2,1)} %reshape.185) | copy-start | bytes 10616836
  451.1 18.3 %slice-start.1 = ((s8[4718592]{0:T(1024)(128)(4,1)}), s8[524288]{0:T(1024)(128)(4,1)S(1)}, s32[]{:S(2)}) async-start(s8[4718592]{0:T(1024)(128)(4,1)} %bitcast.60), calls=%async_computation.13 | async-start | bytes 1048576
  469.4 41.9 %copy-start.2 = (f32[1024,768]{1,0:T(8,128)S(1)}, f32[1024,768]{1,0:T(8,128)}, u32[]{:S(2)}) copy-start(f32[1024,768]{1,0:T(8,128)} %copy-done.1) | copy-start | bytes 9437188
  (26 other events, 109.2 us)
Sparse Core Ops, SparseCore 0:
  11.0 56.8 all-gather.6
  70.8 59.1 all-gather.4
  132.8 62.4 all-gather.8
  198.1 62.4 all-gather.10
  351.5 97.8 reduce-scatter.6
  456.4 118.4 reduce-scatter.4
  581.3 134.6 reduce-scatter.8
  723.5 134.7 reduce-scatter.10
where the time goes:
time: 876 us; the launch traced here: 865 us
  waiting for transfers between devices  469 us (54%)
  matrix products  195 us (22%)
  local copies, waits for them, and re-layouts  102 us (12%)
  other arithmetic  42.8 us (5%)
  blocking collectives  41.1 us (5%)
  between operations  15.2 us (2%)
    reduce_scatter x1, waiting for transfers between devices, body(): lax.psum_scatter(fc2_flat, ('wide', 'narrow'), scatter_dimension=0, tiled...  142 us
    reduce_scatter x1, waiting for transfers between devices, body(): lax.psum_scatter(fc1_flat, ('wide', 'narrow'), scatter_dimension=0, tiled...  141 us
    reduce_scatter x1, waiting for transfers between devices, body(): lax.psum_scatter(qkv_flat, ('wide', 'narrow'), scatter_dimension=0, tiled...  59.3 us
    all_gather x1, waiting for transfers between devices, body(): lax.all_gather(qkv_rows, ('wide', 'narrow'), axis=0, tiled=True)  58.7 us
    all_gather x1, waiting for transfers between devices, body(): lax.all_gather(proj_rows, ('wide', 'narrow'), axis=0, tiled=True)  51.8 us
    psum x1, blocking collectives, body(): lax.psum((gain_grad, norm_bias_grad, qv_bias_grad, proj_bias_grad, fc1_bi...  41.1 us
    dot_general x1, matrix products, body(): jnp.dot(normed_two, fc1_w, preferred_element_type=jnp.float32) + fc1_bias  36.2 us
    dot_general x1, matrix products, body(): jnp.einsum('pqhd,pkhd->phqk', attended_grad, values, preferred_element_ty...  21 us
  transfers between devices with their start and end apart: 8, of which 6 were waited for; matrix products, arithmetic and copies ran while one was open for 28% of the time, Pallas kernels for 0%

commit v1 on v0

v1 whole, which is shorter than its diff:
```python
from functools import partial

import jax
import jax.numpy as jnp
from jax import lax
from jax.experimental import pallas as pl
from jax.experimental.pallas import tpu as pltpu
from jax.sharding import PartitionSpec as P

H = 12
PREFIX = 5
EPSILON = 1e-06
NEGATIVE = -1e30
AXES = ("wide", "narrow")
COLUMNS = 8
BF16 = jnp.bfloat16
F32 = jnp.float32


def dot(a, b):
    return lax.dot_general(a, b, (((1,), (0,)), ((), ())), preferred_element_type=F32)


def dot_nt(a, b):
    return lax.dot_general(a, b, (((1,), (1,)), ((), ())), preferred_element_type=F32)


def dot_tn(a, b):
    return lax.dot_general(a, b, (((0,), (0,)), ((), ())), preferred_element_type=F32)


def params(mib=48):
    return pltpu.CompilerParams(vmem_limit_bytes=mib * 2**20)


def full(shape):
    return pl.BlockSpec(shape, lambda *_: (0,) * len(shape))


def standardize(v):
    centered = v - jnp.mean(v, axis=-1, keepdims=True)
    inverse = lax.rsqrt(jnp.mean(centered * centered, axis=-1, keepdims=True) + EPSILON)
    return centered * inverse, inverse


def standardize_back(grad, scaled, inverse):
    return inverse * (
        grad
        - jnp.mean(grad, axis=-1, keepdims=True)
        - scaled * jnp.mean(grad * scaled, axis=-1, keepdims=True)
    )


def length_of(grid_ref, image):
    return PREFIX + grid_ref[2 * image] * grid_ref[2 * image + 1]


def spans(grid_ref, pack, images):
    found, start = [], 0
    for i in range(images):
        length = length_of(grid_ref, pack * images + i)
        found.append((start, length))
        start = start + length
    return found


def join(scr, core, own, other):
    for i in range(scr.shape[0]):
        scr[i, core] = own[i]
        scr[i, 1 - core] = other[i]
    blocks, cores, rows, columns = scr.shape
    return scr[...].reshape(blocks * cores * rows, columns)


def part(core, matrix, own, other):
    blocks, rows, columns = own.shape
    cut = matrix.reshape(blocks, 2, rows, columns)
    own[...] = jnp.where(core == 0, cut[:, 0], cut[:, 1])
    other[...] = jnp.where(core == 0, cut[:, 1], cut[:, 0])


def prepare_kernel(grid_ref, tok, cot, gain, bias, ls, x, n1, up, b2g, sums, *, images):
    pack = pl.program_id(0)
    slot = tok.shape[0] // images
    row = lax.broadcasted_iota(jnp.int32, (slot, tok.shape[0]), 0)
    column = lax.broadcasted_iota(jnp.int32, (slot, tok.shape[0]), 1)
    total = jnp.zeros((1, tok.shape[1]), F32)
    for i, (start, length) in enumerate(spans(grid_ref, pack, images)):
        place = jnp.where((column - row == start) & (row < length), 1.0, 0.0).astype(BF16)
        rows = pl.ds(i * slot, slot)
        moved = dot(place, tok[...])
        x[rows] = moved.astype(BF16)
        scaled, _ = standardize(moved)
        n1[rows] = (scaled * gain[0:1] + bias[0:1]).astype(BF16)
        upstream = dot(place, cot[...])
        up[rows] = upstream.astype(BF16)
        low = (ls[1:2] * upstream).astype(BF16)
        b2g[rows] = low
        total = total + jnp.sum(low.astype(F32), axis=0, keepdims=True)

    @pl.when(pack == 0)
    def _():
        sums[...] = jnp.zeros_like(sums)

    sums[...] += total


def unplace(grid_ref, pack, images, size):
    slot = size // images
    row = lax.broadcasted_iota(jnp.int32, (size, slot), 0)
    column = lax.broadcasted_iota(jnp.int32, (size, slot), 1)
    return jnp.concatenate(
        [
            jnp.where((row - column == start) & (column < length), 1.0, 0.0).astype(BF16)
            for start, length in spans(grid_ref, pack, images)
        ],
        axis=1,
    )


def lanes(rows, width, head):
    return lax.broadcasted_iota(jnp.int32, (rows, width), 1) < head


def stacked(v, low):
    zero = jnp.zeros_like(v)
    return jnp.concatenate([jnp.where(low, v, zero), jnp.where(low, zero, v)], axis=0)


def softmax(scores, column_ok):
    masked = jnp.where(column_ok, scores, NEGATIVE)
    exponent = jnp.exp(masked - jnp.max(masked, axis=1, keepdims=True))
    return exponent * (1.0 / jnp.sum(exponent, axis=1, keepdims=True))


def attend_kernel(grid_ref, sc, n1, own, other, offset, proj, att, scr, *, slot, head):
    step = pl.program_id(0)
    width = n1.shape[1]
    per = n1.shape[0] // slot
    pair = 2 * head

    @pl.when(step == 0)
    def _():
        join(scr, sc[0], own, other)

    w = scr[...].reshape(width, 3 * width)
    proj[...] = (dot(n1[...], w) + offset[...]).astype(BF16)
    low = lanes(slot, pair, head)
    key_at = lax.broadcasted_iota(jnp.int32, (slot, slot), 1)
    for i in range(per):
        ok = key_at < length_of(grid_ref, step * per + i)
        rows = pl.ds(i * slot, slot)
        for j in range(width // pair):
            q, k, v = (proj[rows, pl.ds(t * width + j * pair, pair)] for t in range(3))
            scores = dot_nt(q, stacked(k, low)) * head ** (-0.5)
            p0 = softmax(scores[:, :slot], ok)
            p1 = softmax(scores[:, slot:], ok)
            p = jnp.concatenate([p0, p1], axis=1).astype(BF16)
            att[rows, pl.ds(j * pair, pair)] = dot(p, stacked(v, low)).astype(BF16)


def hidden_kernel(sc, att, x, b2g, gain, bias, ls, proj_bias, fc1_bias, po, ps, fo, fs, b1, n2, act, slope, go, gs, pscr, fscr, *, tile):
    core = sc[0]

    @pl.when(pl.program_id(0) == 0)
    def _():
        w = join(pscr, core, po, ps)
        for r in range(0, att.shape[0], tile):
            rows = pl.ds(r, tile)
            branch = dot(att[rows], w) + proj_bias[...]
            b1[rows] = branch
            scaled, _ = standardize(x[rows].astype(F32) + ls[0:1] * branch)
            n2[rows] = (scaled * gain[1:2] + bias[1:2]).astype(BF16)

    w = join(fscr, core, fo, fs)
    for r in range(0, att.shape[0], tile):
        rows = pl.ds(r, tile)
        hidden = dot(n2[rows], w) + fc1_bias[...]
        normal = 0.5 * (1.0 + lax.erf(hidden * 0.5**0.5))
        act[rows] = (hidden * normal).astype(BF16)
        slope[rows] = normal + hidden * ((0.5 / jnp.pi) ** 0.5 * jnp.exp(-0.5 * hidden * hidden))
    part(core, dot_tn(act[...], b2g[...]).astype(BF16), go, gs)


def hidden_back_kernel(sc, b2g, n2, slope, wo, ws, hg, sums, go, gs, scr, *, tile):
    core = sc[0]
    w = join(scr, core, wo, ws)
    total = jnp.zeros(sums.shape, F32)
    for r in range(0, b2g.shape[0], tile):
        rows = pl.ds(r, tile)
        low = (dot_nt(b2g[rows], w) * slope[rows]).astype(BF16)
        hg[rows] = low
        total = total + jnp.sum(low.astype(F32), axis=0, keepdims=True)
    sums[...] = total
    part(core, dot_tn(n2[...], hg[...]).astype(BF16), go, gs)


def middle_back_kernel(sc, hg, fo, fs, po, ps, b1, x, up, gain, ls, mg, b1g, ag, sums, acc, fscr, pscr, *, tile):
    core = sc[0]
    step = pl.program_id(0)
    w = join(fscr, core, fo, fs)

    @pl.when(step == 0)
    def _():
        acc[...] = dot_nt(hg[...], w)

    @pl.when(step > 0)
    def _():
        acc[...] += dot_nt(hg[...], w)

    @pl.when(step == pl.num_programs(0) - 1)
    def _():
        wp = join(pscr, core, po, ps)
        totals = [jnp.zeros((1, x.shape[1]), F32) for _ in range(4)]
        for r in range(0, x.shape[0], tile):
            rows = pl.ds(r, tile)
            branch = b1[rows]
            scaled, inverse = standardize(x[rows].astype(F32) + ls[0:1] * branch)
            grad = acc[rows]
            back = up[rows].astype(F32) + standardize_back(grad * gain[1:2], scaled, inverse)
            mg[rows] = back
            low = (ls[0:1] * back).astype(BF16)
            b1g[rows] = low
            ag[rows] = dot_nt(low, wp).astype(BF16)
            terms = (back * branch, low.astype(F32), grad * scaled, grad)
            totals = [t + jnp.sum(v, axis=0, keepdims=True) for t, v in zip(totals, terms)]
        sums[...] = jnp.concatenate(totals, axis=0)


def attend_back_kernel(grid_ref, proj, ag, pg, sums, *, slot, head):
    step = pl.program_id(0)
    width = ag.shape[1]
    per = ag.shape[0] // slot
    pair = 2 * head
    factor = head ** (-0.5)
    low = lanes(slot, pair, head)
    key_at = lax.broadcasted_iota(jnp.int32, (slot, slot), 1)
    for i in range(per):
        ok = key_at < length_of(grid_ref, step * per + i)
        rows = pl.ds(i * slot, slot)
        for j in range(width // pair):
            q, k, v = (proj[rows, pl.ds(t * width + j * pair, pair)] for t in range(3))
            out = ag[rows, pl.ds(j * pair, pair)]
            k2 = stacked(k, low)
            scores = dot_nt(q, k2) * factor
            pull = dot_nt(out, stacked(v, low))
            ps, ss = [], []
            for half in (slice(0, slot), slice(slot, 2 * slot)):
                p = softmax(scores[:, half], ok)
                g = pull[:, half]
                ps.append(p)
                ss.append(p * (g - jnp.sum(g * p, axis=1, keepdims=True)))
            p = jnp.concatenate(ps, axis=1).astype(BF16)
            s = jnp.concatenate(ss, axis=1).astype(BF16)
            dq = dot(s, k2) * factor
            dk = dot_tn(s, q) * factor
            dv = dot_tn(p, out)
            dk = jnp.where(low, dk[:slot], dk[slot:])
            dv = jnp.where(low, dv[:slot], dv[slot:])
            for t, d in enumerate((dq, dk, dv)):
                pg[rows, pl.ds(t * width + j * pair, pair)] = d.astype(BF16)

    @pl.when(step == 0)
    def _():
        sums[...] = jnp.zeros_like(sums)

    sums[...] += jnp.sum(pg[...].astype(F32), axis=0, keepdims=True)


def weight_kernel(sc, n1, att, pg, b1g, go, gs):
    step = pl.program_id(0)
    last = pl.num_programs(0) - 1

    @pl.when(step < last)
    def _():
        part(sc[0], dot_tn(n1[...], pg[...]).astype(BF16), go, gs)

    @pl.when(step == last)
    def _():
        part(sc[0], dot_tn(att[...], b1g[...]).astype(BF16), go, gs)


def input_back_kernel(grid_ref, sc, pg, own, other, x, mg, gain, out, sums, scr, *, images):
    pack = pl.program_id(0)

    @pl.when(pack == 0)
    def _():
        join(scr, sc[0], own, other)
        sums[...] = jnp.zeros_like(sums)

    width = x.shape[1]
    grad = dot_nt(pg[...], scr[...].reshape(width, 3 * width))
    scaled, inverse = standardize(x[...].astype(F32))
    back = mg[...] + standardize_back(grad * gain[0:1], scaled, inverse)
    sums[...] += jnp.concatenate(
        [jnp.sum(grad * scaled, axis=0, keepdims=True), jnp.sum(grad, axis=0, keepdims=True)], axis=0
    )
    place = unplace(grid_ref, pack, images, x.shape[0])
    high = back.astype(BF16)
    rest = back - high.astype(F32)
    mid = rest.astype(BF16)
    lowest = (rest - mid.astype(F32)).astype(BF16)
    out[...] = dot(place, high) + dot(place, mid) + dot(place, lowest)


def layer_out_kernel(grid_ref, sc, act, wo, ws, x, b1, up, ls, fc2_bias, out, sums, acc, scr, *, images):
    step = pl.program_id(0)
    w = join(scr, sc[0], wo, ws)

    @pl.when(step == 0)
    def _():
        acc[...] = dot(act[...], w)

    @pl.when(step > 0)
    def _():
        acc[...] += dot(act[...], w)

    @pl.when(step == pl.num_programs(0) - 1)
    def _():
        size = out.shape[0] // (grid_ref.shape[0] // (2 * images))
        total = jnp.zeros(sums.shape, F32)
        for pack in range(out.shape[0] // size):
            rows = pl.ds(pack * size, size)
            branch = acc[rows] + fc2_bias[...]
            total = total + jnp.sum(up[rows].astype(F32) * branch, axis=0, keepdims=True)
            middle = x[rows].astype(F32) + ls[0:1] * b1[rows]
            result = (middle + ls[1:2] * branch).astype(BF16)
            place = unplace(grid_ref, pack, images, size)
            out[rows] = dot(place, result).astype(BF16)
        sums[...] = total


def gather(block, core):
    whole = lax.all_gather(block, AXES, axis=0, tiled=True)
    cut = whole.reshape(COLUMNS, 2, whole.shape[0] // (2 * COLUMNS), whole.shape[1])
    return cut[:, 0], cut[:, 1]


def scatter(own, other):
    matrix = jnp.stack([own, other], axis=1).reshape(-1, own.shape[-1])
    return lax.psum_scatter(matrix, AXES, scatter_dimension=0, tiled=True).astype(F32)


def reduce_all(v):
    return lax.psum(v, AXES)


def body(
    tokens,
    patch_grid,
    qkv_rows,
    proj_rows,
    fc1_rows,
    fc2_rows,
    norm_gain,
    norm_bias,
    qv_bias,
    proj_bias,
    fc1_bias,
    fc2_bias,
    layer_scale,
    cotangent,
):
    rows, width = tokens.shape
    packs, images, _ = patch_grid.shape
    pack = rows // packs
    slot = pack // images
    head = width // H
    hidden = fc1_bias.shape[0]
    row_width = qkv_rows.shape[1]
    tiles = hidden // width
    tile = min(256, rows)
    sc = jnp.zeros((1,), jnp.int32)
    grid_flat = patch_grid.reshape(-1)
    s = jax.ShapeDtypeStruct
    qkv_own, qkv_other = gather(qkv_rows.reshape(-1, 3 * width), sc)
    both = jnp.concatenate([proj_rows.reshape(-1, width), fc1_rows.reshape(-1, hidden)], axis=1)
    pf_own, pf_other = gather(both, sc)
    fc2_own, fc2_other = gather(fc2_rows.reshape(-1, width), sc)
    thin, wide_rows = width // (2 * COLUMNS), hidden // (2 * COLUMNS)
    per_tile = COLUMNS // tiles

    by_pack = pl.BlockSpec((pack, width), lambda i, *_: (i, 0))
    vec2 = full((2, width))
    x, n1, up, b2g, fc2_sums = pl.pallas_call(
        partial(prepare_kernel, images=images),
        grid_spec=pltpu.PrefetchScalarGridSpec(
            num_scalar_prefetch=1,
            grid=(packs,),
            in_specs=[by_pack, by_pack, vec2, vec2, vec2],
            out_specs=[by_pack] * 4 + [full((1, width))],
        ),
        out_shape=[s((rows, width), BF16)] * 4 + [s((1, width), F32)],
        compiler_params=params(),
    )(grid_flat, tokens, cotangent, norm_gain, norm_bias, layer_scale)

    offset = jnp.concatenate([qv_bias[0], jnp.zeros_like(qv_bias[0]), qv_bias[1]])[None]
    by_tile = lambda w: pl.BlockSpec((tile, w), lambda i, *_: (i, 0))
    proj, att = pl.pallas_call(
        partial(attend_kernel, slot=slot, head=head),
        grid_spec=pltpu.PrefetchScalarGridSpec(
            num_scalar_prefetch=2,
            grid=(rows // tile,),
            in_specs=[by_tile(width), full((COLUMNS, thin, 3 * width)), full((COLUMNS, thin, 3 * width)), full((1, 3 * width))],
            out_specs=[by_tile(3 * width), by_tile(width)],
            scratch_shapes=[pltpu.VMEM((COLUMNS, 2, thin, 3 * width), BF16)],
        ),
        out_shape=[s((rows, 3 * width), BF16), s((rows, width), BF16)],
        compiler_params=params(),
    )(grid_flat, sc, n1, qkv_own, qkv_other, offset)

    whole = full((rows, width))
    proj_blocks = pl.BlockSpec((COLUMNS, thin, width), lambda i, *_: (0, 0, 0))
    fc1_blocks = pl.BlockSpec((COLUMNS, thin, width), lambda i, *_: (0, 0, 1 + i))
    fc2_blocks = pl.BlockSpec((per_tile, wide_rows, width), lambda i, *_: (i, 0, 0))
    hidden_tile = pl.BlockSpec((rows, width), lambda i, *_: (0, i))
    thin_scr = pltpu.VMEM((COLUMNS, 2, thin, width), BF16)
    wide_scr = pltpu.VMEM((per_tile, 2, wide_rows, width), BF16)
    vec1 = full((1, width))
    hidden_vec = pl.BlockSpec((1, width), lambda i, *_: (0, i))
    b1, n2, act, slope, fc2g_own, fc2g_other = pl.pallas_call(
        partial(hidden_kernel, tile=tile),
        grid_spec=pltpu.PrefetchScalarGridSpec(
            num_scalar_prefetch=1,
            grid=(tiles,),
            in_specs=[whole, whole, whole, vec2, vec2, vec2, vec1, hidden_vec, proj_blocks, proj_blocks, fc1_blocks, fc1_blocks],
            out_specs=[whole, whole, hidden_tile, hidden_tile, fc2_blocks, fc2_blocks],
            scratch_shapes=[thin_scr, thin_scr],
        ),
        out_shape=[s((rows, width), F32), s((rows, width), BF16), s((rows, hidden), BF16), s((rows, hidden), F32)]
        + [s((COLUMNS, wide_rows, width), BF16)] * 2,
        compiler_params=params(56),
    )(sc, att, x, b2g, norm_gain, norm_bias, layer_scale, proj_bias[None], fc1_bias[None], pf_own, pf_other, pf_own, pf_other)
    fc2_grad = scatter(fc2g_own, fc2g_other)

    column_blocks = pl.BlockSpec((COLUMNS, thin, width), lambda i, *_: (0, 0, i))
    hg, fc1_sums, fc1g_own, fc1g_other = pl.pallas_call(
        partial(hidden_back_kernel, tile=tile),
        grid_spec=pltpu.PrefetchScalarGridSpec(
            num_scalar_prefetch=1,
            grid=(tiles,),
            in_specs=[whole, whole, hidden_tile, fc2_blocks, fc2_blocks],
            out_specs=[hidden_tile, hidden_vec, column_blocks, column_blocks],
            scratch_shapes=[wide_scr],
        ),
        out_shape=[s((rows, hidden), BF16), s((1, hidden), F32)] + [s((COLUMNS, thin, hidden), BF16)] * 2,
        compiler_params=params(56),
    )(sc, b2g, n2, slope, fc2_own, fc2_other)
    fc1_grad = scatter(fc1g_own, fc1g_other)

    mg, b1g, ag, middle_sums = pl.pallas_call(
        partial(middle_back_kernel, tile=tile),
        grid_spec=pltpu.PrefetchScalarGridSpec(
            num_scalar_prefetch=1,
            grid=(tiles,),
            in_specs=[hidden_tile, fc1_blocks, fc1_blocks, proj_blocks, proj_blocks, whole, whole, whole, vec2, vec2],
            out_specs=[whole, whole, whole, full((4, width))],
            scratch_shapes=[pltpu.VMEM((rows, width), F32), thin_scr, thin_scr],
        ),
        out_shape=[s((rows, width), F32), s((rows, width), BF16), s((rows, width), BF16), s((4, width), F32)],
        compiler_params=params(56),
    )(sc, hg, pf_own, pf_other, pf_own, pf_other, b1, x, up, norm_gain, layer_scale)

    pg, proj_sums = pl.pallas_call(
        partial(attend_back_kernel, slot=slot, head=head),
        grid_spec=pltpu.PrefetchScalarGridSpec(
            num_scalar_prefetch=1,
            grid=(rows // tile,),
            in_specs=[by_tile(3 * width), by_tile(width)],
            out_specs=[by_tile(3 * width), full((1, 3 * width))],
        ),
        out_shape=[s((rows, 3 * width), BF16), s((1, 3 * width), F32)],
        compiler_params=params(),
    )(grid_flat, proj, ag)

    qp_own, qp_other = pl.pallas_call(
        weight_kernel,
        grid_spec=pltpu.PrefetchScalarGridSpec(
            num_scalar_prefetch=1,
            grid=(4,),
            in_specs=[whole, whole, pl.BlockSpec((rows, width), lambda i, *_: (0, jnp.minimum(i, 2))), whole],
            out_specs=[column_blocks, column_blocks],
        ),
        out_shape=[s((COLUMNS, thin, 4 * width), BF16)] * 2,
        compiler_params=params(),
    )(sc, n1, att, pg, b1g)
    qp_grad = scatter(qp_own, qp_other)

    input_grad, input_sums = pl.pallas_call(
        partial(input_back_kernel, images=images),
        grid_spec=pltpu.PrefetchScalarGridSpec(
            num_scalar_prefetch=2,
            grid=(packs,),
            in_specs=[pl.BlockSpec((pack, 3 * width), lambda i, *_: (i, 0)), full((COLUMNS, thin, 3 * width)), full((COLUMNS, thin, 3 * width)), by_pack, by_pack, vec2],
            out_specs=[by_pack, vec2],
            scratch_shapes=[pltpu.VMEM((COLUMNS, 2, thin, 3 * width), BF16)],
        ),
        out_shape=[s((rows, width), F32), s((2, width), F32)],
        compiler_params=params(),
    )(grid_flat, sc, pg, qkv_own, qkv_other, x, mg, norm_gain)

    layer_out, out_sums = pl.pallas_call(
        partial(layer_out_kernel, images=images),
        grid_spec=pltpu.PrefetchScalarGridSpec(
            num_scalar_prefetch=2,
            grid=(tiles,),
            in_specs=[hidden_tile, fc2_blocks, fc2_blocks, whole, whole, whole, vec2, vec1],
            out_specs=[whole, vec1],
            scratch_shapes=[pltpu.VMEM((rows, width), F32), wide_scr],
        ),
        out_shape=[s((rows, width), BF16), s((1, width), F32)],
        compiler_params=params(),
    )(grid_flat, sc, act, fc2_own, fc2_other, x, b1, up, layer_scale, fc2_bias[None])

    sums = jnp.concatenate(
        [
            input_sums[0:1],
            middle_sums[2:3],
            input_sums[1:2],
            middle_sums[3:4],
            proj_sums[:, :width],
            proj_sums[:, 2 * width :],
            middle_sums[1:2],
            fc2_sums,
            middle_sums[0:1],
            out_sums,
            fc1_sums.reshape(tiles, width),
        ],
        axis=0,
    )
    sums = reduce_all(sums)
    return (
        layer_out,
        input_grad,
        qp_grad[:, : 3 * width].reshape(-1, row_width),
        qp_grad[:, 3 * width :].reshape(-1, row_width),
        fc1_grad.reshape(-1, row_width),
        fc2_grad.reshape(-1, row_width),
        sums[0:2],
        sums[2:4],
        sums[4:6],
        sums[6],
        sums[10:].reshape(-1),
        sums[7],
        sums[8:10],
    )


def solution(mesh):
    split = P(AXES, None)
    return jax.shard_map(
        body,
        mesh=mesh,
        in_specs=(split, P(AXES, None, None)) + (split,) * 4 + (P(),) * 7 + (split,),
        out_specs=(split,) * 6 + (P(),) * 7,
        check_vma=False,
    )
```

time: 876 us -> 669 us (0.76)
  matrix products: 195 us -> 0 us
  Pallas kernels: 0 us -> 147 us
  waiting for transfers between devices: 469 us -> 395 us
  local copies, waits for them, and re-layouts: 102 us -> 57 us
  other arithmetic: 42.8 us -> 8.42 us
    dot_general x18 -> x0, matrix products: 195 us -> none  [the longest x1 36.2 us: body(): jnp.dot(normed_two, fc1_w, preferred_element_type=jnp.float32) + fc1_bias]
    pallas_call x0 -> x9, Pallas kernels: none -> 147 us  [the longest x1 27.6 us: body(): pl.pallas_call(partial(attend_back_kernel, slot=slot, head=head), grid_sp...]
    reduce_scatter x4 -> x3, waiting for transfers between devices: 343 us -> 234 us  [scatter(): lax.psum_scatter(matrix, AXES, scatter_dimension=0, tiled=True).astype(F32)]
    reshape x12 -> x11, local copies, waits for them, and re-layouts: 75 us -> 10.7 us  [the longest x1 1.76 us: body(): fc2_grad.reshape(-1, row_width)]
    all_gather x4 -> x3, waiting for transfers between devices: 124 us -> 161 us  [gather(): whole = lax.all_gather(block, AXES, axis=0, tiled=True)]
    convert_element_type x1 -> x0, other arithmetic: 18.1 us -> none  [body(): (probability * (probability_grad - inner_total)).astype(jnp.bfloat16)]
    reduce_sum x8 -> x0, other arithmetic: 18 us -> none  [the longest x1 11.5 us: body(): row_total = jnp.sum(exponent, axis=-1, keepdims=True)]
    squeeze x0 -> x3, local copies, waits for them, and re-layouts: none -> 14 us  [gather(): return (cut[:, 0], cut[:, 1])]
  transfers between devices with their start and end apart: 8 -> 6, of which waited for: 6 -> 6; matrix products, arithmetic and copies ran while one was open for 28% -> 5% of each run, Pallas kernels for 0% -> 7%
where the time goes in v1:
time: 669 us; the launch traced here: 663 us
  waiting for transfers between devices  395 us (59%)
  Pallas kernels  147 us (22%)
  local copies, waits for them, and re-layouts  57 us (9%)
  blocking collectives  40.4 us (6%)
  between operations  14.5 us (2%)
  other arithmetic  8.42 us (1%)
    reduce_scatter x3, waiting for transfers between devices, scatter(): lax.psum_scatter(matrix, AXES, scatter_dimension=0, tiled=True).astype(F32)  234 us
    all_gather x3, waiting for transfers between devices, gather(): whole = lax.all_gather(block, AXES, axis=0, tiled=True)  161 us
    psum x1, blocking collectives, reduce_all(): return lax.psum(v, AXES)  40.4 us
    pallas_call x1, Pallas kernels, body(): pl.pallas_call(partial(attend_back_kernel, slot=slot, head=head), grid_sp...  27.6 us
    pallas_call x1, Pallas kernels, body(): pl.pallas_call(partial(hidden_kernel, tile=tile), grid_spec=pltpu.Prefetc...  21.6 us
    unnamed x45, local copies, waits for them, and re-layouts  18.9 us
    pallas_call x1, Pallas kernels, body(): pl.pallas_call(weight_kernel, grid_spec=pltpu.PrefetchScalarGridSpec(num_...  18.7 us
    pallas_call x1, Pallas kernels, body(): pl.pallas_call(partial(middle_back_kernel, tile=tile), grid_spec=pltpu.Pr...  17.4 us
  transfers between devices with their start and end apart: 6, of which 6 were waited for; matrix products, arithmetic and copies ran while one was open for 5% of the time, Pallas kernels for 7%

profile of v1, /device:TPU:0, one launch (start us, length us, event | category | flops | bytes accessed | tf_op | source)
XLA Modules:
  0.0 663.3 jit_solution(11971709124093647503)
XLA Ops:
  18.4 5.4 shard_map.237
  26.1 48.3 %all-gather.4.cloned.1.call-done = bf16[768,2304]{1,0:T(8,128)(2,1)} async-done(((bf16[24,2304]{1,0:T(8,128)(2,1)}), bf16[768,2304]{1,0:T(8,128)(2,1)}) %all-gather.4.cloned.1.call-update) | async-done | bytes 3538960 | tf_op jit(solution)/shard_map/all_gather | solution.py:334
  74.4 3.4 slice_bitcast_fusion.4
  77.9 12.2 %shard_map.238 = (bf16[1024,2304]{1,0:T(8,128)(2,1)}, bf16[1024,768]{1,0:T(8,128)(2,1)S(1)}) custom-call(s32[16]{0:T(128)S(1)} %reshape.83.grid_ref, s32[1]{0:T(128)} %constant.0.clone.1.sc, bf16[1024,768]{1,0:T(8,128)(2,1)S(1)} %get-tuple-element.42.n1, bf16[8,48,2304]{2,1,0:T(8,128)(2,1)S(1)} %get-tuple-element.80.own, ...), custom_call_target="tpu_custom_call" | custom-call | tf_op jit(solution)/shard_map/pallas_call | solution.py:399
  92.5 47.9 %all-gather.8.cloned.1.call-done = bf16[3072,768]{1,0:T(8,128)(2,1)} async-done(((bf16[96,768]{1,0:T(8,128)(2,1)}), bf16[3072,768]{1,0:T(8,128)(2,1)}) %all-gather.8.cloned.1.call-update) | async-done | bytes 4718608 | tf_op jit(solution)/shard_map/all_gather | solution.py:334
  140.4 4.9 slice_bitcast_fusion.2
  145.3 65.1 %all-gather.6.cloned.1.call-done = bf16[768,3840]{1,0:T(8,128)(2,1)} async-done(((bf16[24,3840]{1,0:T(8,128)(2,1)}), bf16[768,3840]{1,0:T(8,128)(2,1)}) %all-gather.6.cloned.1.call-update) | async-done | bytes 5898256 | tf_op jit(solution)/shard_map/all_gather | solution.py:334
  210.4 5.7 slice_bitcast_fusion
  216.0 21.6 %shard_map.239 = (f32[1024,768]{1,0:T(8,128)}, bf16[1024,768]{1,0:T(8,128)(2,1)}, bf16[1024,3072]{1,0:T(8,128)(2,1)}, f32[1024,3072]{1,0:T(8,128)}, bf16[8,192,7...) custom-call(s32[1]{0:T(128)} %constant.0.clone.1.sc, bf16[1024,768]{1,0:T(8,128)(2,1)} %copy-done.6, ...), custom_call_target="tpu_custom_call" | custom-call | tf_op jit(solution)/shard_map/pallas_call | solution.py:421
  237.6 15.7 %shard_map.241 = (bf16[1024,3072]{1,0:T(8,128)(2,1)}, f32[1,3072]{1,0:T(1,128)}, bf16[8,48,3072]{2,1,0:T(8,128)(2,1)}, bf16[8,48,3072]{2,1,0:T(8,128)(2,1)}) custom-call(s32[1]{0:T(128)} %constant.0.clone.1.sc, bf16[1024,768]{1,0:T(8,128)(2,1)} %get-tuple-element.45.b2g, bf16[1024,768]{1,0:T(8,128)(2,1)} %get-tuple-element.51.n2, ...), custom_call_target="tpu_custom_call" | custom-call | tf_op jit(solution)/shard_map/pallas_call | solution.py:437
  253.4 17.4 %shard_map.242 = (f32[1024,768]{1,0:T(8,128)}, bf16[1024,768]{1,0:T(8,128)(2,1)}, bf16[1024,768]{1,0:T(8,128)(2,1)}, f32[4,768]{1,0:T(4,128)}) custom-call(s32[1]{0:T(128)} %constant.0.clone.1.sc, bf16[1024,3072]{1,0:T(8,128)(2,1)} %get-tuple-element.53.hg, bf16[8,48,3840]{2,1,0:T(8,128)(2,1)} %get-tuple-element.76.po.fo, ...), custom_call_target="tpu_custom_call" | custom-call | tf_op jit(solution)/shard_map/pallas_call | solution.py:451
  272.2 27.6 %shard_map.243 = (bf16[1024,2304]{1,0:T(8,128)(2,1)}, f32[1,2304]{1,0:T(1,128)S(1)}) custom-call(s32[16]{0:T(128)S(1)} %reshape.83.grid_ref, bf16[1024,2304]{1,0:T(8,128)(2,1)} %get-tuple-element.50.proj, bf16[1024,768]{1,0:T(8,128)(2,1)S(1)} %copy-done.11), custom_call_target="tpu_custom_call" | custom-call | tf_op jit(solution)/shard_map/pallas_call | solution.py:464
  299.8 18.7 %shard_map.245 = (bf16[8,48,3072]{2,1,0:T(8,128)(2,1)}, bf16[8,48,3072]{2,1,0:T(8,128)(2,1)}) custom-call(s32[1]{0:T(128)} %constant.0.clone.1.sc, bf16[1024,768]{1,0:T(8,128)(2,1)S(1)} %get-tuple-element.42.n1, bf16[1024,768]{1,0:T(8,128)(2,1)S(1)} %copy-done.7, bf16[1024,2304]{1,0:T(8,128)(2,1)} %get-tuple-element.55.pg, bf16[1024,768]{1,0:T(8,128)(2,1)S(1)} %copy-done.10), custom_call_target="tpu_custom_call" | custom-call | tf_op jit(solution)/shard_map/pallas_call | solution.py:476
  318.5 2.8 pad_maximum_fusion
  321.3 2.6 copy.35
  327.7 2.6 copy.36
  332.0 2.1 pad_maximum_fusion.2
  334.2 2.6 copy.37
  340.3 16.9 %shard_map.244 = (f32[1024,768]{1,0:T(8,128)}, f32[2,768]{1,0:T(2,128)S(1)}) custom-call(s32[16]{0:T(128)S(1)} %reshape.83.grid_ref, s32[1]{0:T(128)} %constant.0.clone.1.sc, bf16[1024,2304]{1,0:T(8,128)(2,1)} %get-tuple-element.55.pg, bf16[8,48,2304]{2,1,0:T(8,128)(2,1)S(1)} %copy-done.5, bf16[8,48,2304]{2,1,0:T(8,128)(2,1)S(1)} %copy-done.3, ...), custom_call_target="tpu_custom_call" | custom-call | tf_op jit(solution)/shard_map/pallas_call | solution.py:489
  361.6 11.9 %shard_map.240 = (bf16[1024,768]{1,0:T(8,128)(2,1)}, f32[1,768]{1,0:T(1,128)S(1)}) custom-call(s32[16]{0:T(128)S(1)} %reshape.83.grid_ref, s32[1]{0:T(128)} %constant.0.clone.1.sc, bf16[1024,3072]{1,0:T(8,128)(2,1)} %get-tuple-element.46.act, bf16[8,192,768]{2,1,0:T(8,128)(2,1)S(1)} %copy-done.2, bf16[8,192,768]{2,1,0:T(8,128)(2,1)} %get-tuple-element.77.ws, ...), custom_call_target="tpu_custom_call" | custom-call | tf_op jit(solution)/shard_map/pallas_call | solution.py:502
  373.6 40.4 %psum.7 = f32[14,768]{1,0:T(8,128)S(1)} all-reduce(f32[14,768]{1,0:T(8,128)S(1)} %concatenate.11), channel_id=1, replica_groups=mesh['wide'=16,'narrow'=2] {'wide','narrow'}, use_global_device_ids=true, to_apply=%region_3.0 | all-reduce | flops 10752 | bytes 86016 | tf_op jit(solution)/shard_map/psum | solution.py:345
  415.9 14.9 %reduce-scatter.4.cloned.1.call-done = bf16[24,3072]{1,0:T(8,128)(2,1)} async-done(((bf16[768,3072]{1,0:T(8,128)(2,1)}), bf16[24,3072]{1,0:T(8,128)(2,1)}) %reduce-scatter.4.cloned.1.call-update) | async-done | bytes 147472 | tf_op jit(solution)/shard_map/reduce_scatter | solution.py:341
  433.8 109.3 %reduce-scatter.6.cloned.1.call-done = bf16[24,3072]{1,0:T(8,128)(2,1)} async-done(((bf16[768,3072]{1,0:T(8,128)(2,1)}), bf16[24,3072]{1,0:T(8,128)(2,1)}) %reduce-scatter.6.cloned.1.call-update) | async-done | bytes 147472 | tf_op jit(solution)/shard_map/reduce_scatter | solution.py:341
  544.8 109.7 %reduce-scatter.8.cloned.1.call-done = bf16[96,768]{1,0:T(8,128)(2,1)} async-done(((bf16[3072,768]{1,0:T(8,128)(2,1)}), bf16[96,768]{1,0:T(8,128)(2,1)}) %reduce-scatter.8.cloned.1.call-update) | async-done | bytes 147472 | tf_op jit(solution)/shard_map/reduce_scatter | solution.py:341
  (86 shorter events, 39.0 us)
Async XLA Ops:
  7.2 67.2 %all-gather.4.cloned.1.call-start = ((), (), s32[]{:S(2)}) async-start(), calls=%async_computation.3 | async-start | bytes 3649536 | tf_op jit(solution)/shard_map/all_gather | solution.py:334
  8.9 131.4 %all-gather.8.cloned.1.call-start = ((), (), s32[]{:S(2)}) async-start(), calls=%async_computation.5 | async-start | bytes 4866048 | tf_op jit(solution)/shard_map/all_gather | solution.py:334
  10.7 199.6 %all-gather.6.cloned.1.call-start = ((), (), s32[]{:S(2)}) async-start(), calls=%async_computation.4 | async-start | bytes 6082560 | tf_op jit(solution)/shard_map/all_gather | solution.py:334
  13.3 417.5 %reduce-scatter.4.cloned.1.call-start = ((), (), s32[]{:S(2)}) async-start(), calls=%async_computation.6 | async-start | bytes 4866048 | tf_op jit(solution)/shard_map/reduce_scatter | solution.py:341
  23.8 1.2 copy-start
  24.9 1.1 copy-start.8
  90.1 1.2 copy-start.4
  91.3 1.2 copy-start.6
  270.8 1.4 copy-start.11
  272.2 27.6 %copy-start.7 = (bf16[1024,768]{1,0:T(8,128)(2,1)S(1)}, bf16[1024,768]{1,0:T(8,128)(2,1)}, u32[]{:S(2)}) copy-start(bf16[1024,768]{1,0:T(8,128)(2,1)} %copy-done.6) | copy-start | bytes 4718596
  272.2 27.6 %copy-start.10 = (bf16[1024,768]{1,0:T(8,128)(2,1)S(1)}, bf16[1024,768]{1,0:T(8,128)(2,1)}, u32[]{:S(2)}) copy-start(bf16[1024,768]{1,0:T(8,128)(2,1)} %get-tuple-element.58.b1g) | copy-start | bytes 4718596
  323.9 1.7 copy-start.18
  323.9 219.2 %reduce-scatter.6.cloned.1.call-start = ((), (), s32[]{:S(2)}) async-start(), calls=%async_computation.7 | async-start | bytes 4866048 | tf_op jit(solution)/shard_map/reduce_scatter | solution.py:341
  330.3 1.7 copy-start.17
  330.3 324.2 %reduce-scatter.8.cloned.1.call-start = ((), (), s32[]{:S(2)}) async-start(), calls=%async_computation.8 | async-start | bytes 4866048 | tf_op jit(solution)/shard_map/reduce_scatter | solution.py:341
  336.8 1.5 copy-start.1
  336.8 2.0 copy-start.3
  336.8 2.0 copy-start.15
  338.8 1.5 copy-start.5
  340.3 17.4 %copy-start.19 = (f32[1,3072]{1,0:T(1,128)S(1)}, f32[1,3072]{1,0:T(1,128)}, u32[]{:S(2)}) copy-start(f32[1,3072]{1,0:T(1,128)} %get-tuple-element.70) | copy-start | bytes 36868
  340.3 18.1 %copy-start.13 = (f32[2,768]{1,0:T(2,128)S(1)}, f32[2,768]{1,0:T(2,128)}, u32[]{:S(2)}) copy-start(f32[2,768]{1,0:T(2,128)} %ls.7) | copy-start | bytes 18436
  358.4 1.7 copy-start.2
  360.1 1.4 copy-start.9
  361.6 11.9 %copy-start.20 = (f32[4,768]{1,0:T(4,128)S(1)}, f32[4,768]{1,0:T(4,128)}, u32[]{:S(2)}) copy-start(f32[4,768]{1,0:T(4,128)} %get-tuple-element.66) | copy-start | bytes 36868
  (4 other events, 2.8 us)
Sparse Core Ops, SparseCore 0:
  11.5 62.8 all-gather.3
  77.9 62.4 all-gather.7
  143.9 66.4 all-gather.5
  324.1 106.6 reduce-scatter.3
  437.0 106.0 reduce-scatter.5
  548.4 106.0 reduce-scatter.7
